TPU v7x, 32 devices: a whole 2x2x4 slice. The times are simulated.
32 devices in a mesh: fsdp: 2 (over x), ctx: 4 (over z), tp: 4 (over y, core).
Axes of the slice: x: 2, y: 2, z: 4, core: 2. Of those that a mesh axis runs over, the one named last changes fastest.
Arguments:
- tokens: bfloat16 [8, 1024, 1536], P('fsdp', 'ctx'), may hold values from -6 to 6
- segment_ids: int32 [8, 1024], P('fsdp', 'ctx'), may hold values from 0 to 1023, as said below
- in_gain: bfloat16 [1536], replicated, may hold values from 0.3984375 to 1.59375
- w_zx: bfloat16 [1536, 2, 3072], P(('fsdp', 'ctx'), None, 'tp'), may hold values from -0.15625 to 0.15625
- w_bc: bfloat16 [1536, 256], P(('fsdp', 'ctx')), may hold values from -0.15625 to 0.15625
- w_dt: bfloat16 [1536, 48], P(('fsdp', 'ctx'), 'tp'), may hold values from -0.15625 to 0.15625
- dt_bias: float32 [48], P('tp'), may hold values from -6 to -3
- a_log: float32 [48], P('tp'), may hold values from -0.5 to 2.5
- skip_gain: float32 [48], P('tp'), may hold values from 0.5 to 2
- conv_x: bfloat16 [4, 3072], P(None, 'tp'), may hold values from -3 to 3
- conv_x_bias: bfloat16 [3072], P('tp'), may hold values from -0.5 to 0.5
- conv_bc: bfloat16 [4, 256], replicated, may hold values from -3 to 3
- conv_bc_bias: bfloat16 [256], replicated, may hold values from -0.5 to 0.5
- gate_gain: bfloat16 [3072], P('tp'), may hold values from 0.3984375 to 1.59375
- w_out: bfloat16 [3072, 1536], P('tp', ('fsdp', 'ctx')), may hold values from -0.109375 to 0.109375
- cotangent: bfloat16 [8, 1024, 1536], P('fsdp', 'ctx'), may hold values from -6 to 6
Outputs:
- mixed: bfloat16 [8, 1024, 1536], P('fsdp', 'ctx', 'tp')
- grad_tokens: float32 [8, 1024, 1536], P('fsdp', 'ctx', 'tp')
- grad_in_gain: float32 [1536], P('tp')
- grad_w_zx: float32 [1536, 2, 3072], P(('fsdp', 'ctx'), None, 'tp')
- grad_w_bc: float32 [1536, 256], P(('fsdp', 'ctx'))
- grad_w_dt: float32 [1536, 48], P(('fsdp', 'ctx'), 'tp')
- grad_dt_bias: float32 [48], P('tp')
- grad_a_log: float32 [48], P('tp')
- grad_skip_gain: float32 [48], P('tp')
- grad_conv_x: float32 [4, 3072], P(None, 'tp')
- grad_conv_x_bias: float32 [3072], P('tp')
- grad_conv_bc: float32 [4, 256], replicated
- grad_conv_bc_bias: float32 [256], replicated
- grad_gate_gain: float32 [3072], P('tp')
- grad_w_out: float32 [3072, 1536], P('tp', ('fsdp', 'ctx'))
Inputs may be any that keep to these rules, and one draw needn't show every extreme that they name: segment_ids[s, t] is the position within sequence s at which the document holding token t begins: it never exceeds t, never falls along t, equals 0 at t = 0, and equals t exactly where a document begins. In each aligned group of 4 sequences, one sequence holds a document that begins within its first 256 positions and ends within its last 256.
All inputs are finite; a program needn't handle non-finite values.
Results may differ from a plain program's by a relative error of at most 0.01.
Values may be sent and summed in bfloat16 or wider, within the bound.
No kernel may reach another device: no remote copies, remote signals or barrier semaphores. Data moves between devices by JAX's collectives and lax.ppermute only.
A program may use at most 192 MiB of HBM per device.

v0:
```python
import jax
import jax.numpy as jnp
from jax import lax
from jax.sharding import PartitionSpec as P

D = 1536
HEADDIM = 64
STATE = 128
CONV = 4
INNER = 3072


norm_eps = 1e-05


def shifted(value, axis, steps):
    count = lax.axis_size(axis)
    initial, last = (max(0, -steps), min(count, count - steps))
    return lax.ppermute(value, axis, [(source, source + steps) for source in range(initial, last)])


def entering(part, axis, combine, identity, reverse):
    count = lax.axis_size(axis)
    place = lax.axis_index(axis)
    ahead = count - 1 - place if reverse else place
    gathered = jax.tree.map(lambda a: lax.all_gather(a, axis), part)
    state = jax.tree.map(lambda a, e: jnp.zeros_like(a) + jnp.asarray(e, a.dtype), part, identity)

    def one(step, state):
        source = count - 1 - step if reverse else step
        return combine(
            state, jax.tree.map(lambda a: lax.dynamic_index_in_dim(a, source, 0, False), gathered)
        )

    return lax.fori_loop(0, ahead, one, state)


def as_sent(x):
    return jax.tree.map(lambda a: a.astype(jnp.bfloat16) if a.dtype == jnp.float32 else a, x)


def conv_apply(u_val, rim_val, weight, bias_val, seg_ids, positions):
    extended = jnp.concatenate([rim_val, u_val], axis=1)
    tap_count = weight.shape[0]
    length = u_val.shape[1]
    conv_sum = jnp.zeros_like(u_val) + bias_val[None, None, :]
    for tap_index in range(tap_count):
        lag_size = tap_count - 1 - tap_index
        window = extended[:, tap_index : tap_index + length, :]
        usable = (seg_ids <= positions[None, :] - lag_size).astype(u_val.dtype)
        conv_sum = conv_sum + weight[tap_index][None, None, :] * window * usable[:, :, None]
    return conv_sum


def ssd_parts(x_heads, b_mat, c_mat, dt_val, log_decay, seg_ids, positions):
    highest = lax.Precision.HIGHEST
    cum_decay = jnp.cumsum(log_decay, axis=1)
    lower_tri = positions[:, None] >= positions[None, :]
    same_doc = (seg_ids[:, :, None] == seg_ids[:, None, :]) & lower_tri[None, :, :]
    same_float = same_doc.astype(log_decay.dtype)[..., None]
    log_gap = cum_decay[:, :, None, :] - cum_decay[:, None, :, :]
    decay_mat = jnp.exp(jnp.where(same_doc[..., None], log_gap, 0.0)) * same_float
    scores = jnp.einsum("btn,bsn->bts", c_mat, b_mat, precision=highest)
    weights = decay_mat * scores[..., None] * dt_val[:, None, :, :]
    y_local = jnp.einsum("btsh,bshp->bthp", weights, x_heads, precision=highest)
    block_start = positions[0]
    carried = (seg_ids < block_start).astype(log_decay.dtype)
    into_scale = jnp.exp(cum_decay) * carried[..., None]
    last_doc = (seg_ids == seg_ids[:, -1:]).astype(log_decay.dtype)
    tail_scale = jnp.exp(cum_decay[:, -1:, :] - cum_decay) * last_doc[..., None]
    state_local = jnp.einsum(
        "bsh,bshp,bsn->bhpn", tail_scale * dt_val, x_heads, b_mat, precision=highest
    )
    decay_total = jnp.exp(cum_decay[:, -1, :]) * carried[:, -1:]
    return (y_local, into_scale, decay_total, state_local)


def chain_pair(earlier, later):
    early_dec, early_state = earlier
    late_dec, late_state = later
    return (early_dec * late_dec, late_dec[..., None, None] * early_state + late_state)


def per_device(
    tokens,
    segment_ids,
    in_gain,
    w_zx,
    w_bc,
    w_dt,
    dt_bias,
    a_log,
    skip_gain,
    conv_x,
    conv_x_bias,
    conv_bc,
    conv_bc_bias,
    gate_gain,
    w_out,
    cotangent,
):
    highest = lax.Precision.HIGHEST
    single = jnp.float32
    tp_count = lax.axis_size("tp")
    tp_rank = lax.axis_index("tp")
    ctx_rank = lax.axis_index("ctx")
    seqs_here, block_len, width = tokens.shape
    inner_here = w_zx.shape[2]
    heads_here = w_dt.shape[1]
    slice_width = width // tp_count
    rim_len = CONV - 1
    positions = ctx_rank * block_len + jnp.arange(block_len, dtype=jnp.int32)
    full_zx, full_bc, full_dt, full_out = (
        lax.all_gather(w_zx, ("fsdp", "ctx"), axis=0, tiled=True),
        lax.all_gather(w_bc, ("fsdp", "ctx"), axis=0, tiled=True),
        lax.all_gather(w_dt, ("fsdp", "ctx"), axis=0, tiled=True),
        lax.all_gather(w_out, ("fsdp", "ctx"), axis=1, tiled=True),
    )
    x_float = tokens.astype(single)
    inv_rms = lax.rsqrt(jnp.mean(x_float * x_float, axis=-1, keepdims=True) + norm_eps)
    x_hat = x_float * inv_rms
    normed = (x_hat * in_gain.astype(single)).astype(jnp.bfloat16)
    zx_both = jnp.einsum("scd,dkf->sckf", normed, full_zx, preferred_element_type=single)
    z_part = zx_both[:, :, 0]
    x_part = zx_both[:, :, 1]
    bc_part = jnp.einsum("scd,dn->scn", normed, full_bc, preferred_element_type=single)
    dt_raw = jnp.einsum("scd,dh->sch", normed, full_dt, preferred_element_type=single)
    u_in = jnp.concatenate([x_part, bc_part], axis=-1)
    rim_rows = shifted(u_in[:, block_len - rim_len :, :].astype(jnp.bfloat16), "ctx", 1).astype(
        jnp.float32
    )
    conv_weight = jnp.concatenate([conv_x, conv_bc], axis=1).astype(single)
    conv_bias = jnp.concatenate([conv_x_bias, conv_bc_bias]).astype(single)

    def pre_mix(u_val, rim_val, weight, bias_val):
        return jax.nn.silu(conv_apply(u_val, rim_val, weight, bias_val, segment_ids, positions))

    activated, pre_pull = jax.vjp(pre_mix, u_in, rim_rows, conv_weight, conv_bias)
    x_heads = activated[..., :inner_here].reshape(seqs_here, block_len, heads_here, HEADDIM)
    b_mat = activated[..., inner_here : inner_here + STATE]
    c_mat = activated[..., inner_here + STATE :]

    def local_ssd(heads_in, b_in, c_in, raw_in, bias_in, alog_in):
        dt_val = jax.nn.softplus(raw_in + bias_in)
        log_decay = -dt_val * jnp.exp(alog_in)
        return ssd_parts(heads_in, b_in, c_in, dt_val, log_decay, segment_ids, positions)

    (y_local, into_scale, decay_total, state_local), ssd_pull = jax.vjp(
        local_ssd, x_heads, b_mat, c_mat, dt_raw, dt_bias, a_log
    )
    identity = (jnp.ones_like(decay_total), jnp.zeros_like(state_local))
    _, state_in = entering((decay_total, state_local), "ctx", chain_pair, identity, False)
    carried_read = jnp.einsum("btn,bhpn->bthp", c_mat, state_in, precision=highest)
    skip_wide = skip_gain[None, None, :, None]
    y_heads = y_local + into_scale[..., None] * carried_read + skip_wide * x_heads
    y_flat = y_heads.reshape(seqs_here, block_len, inner_here)
    gate_sig = jax.nn.sigmoid(z_part)
    gated_val = y_flat * (z_part * gate_sig)
    row_sq = lax.psum(jnp.sum(gated_val * gated_val, axis=-1), "tp")
    inv_gate = lax.rsqrt(row_sq / INNER + norm_eps)[..., None]
    gate_wide = gate_gain.astype(single)
    hidden = (gated_val * inv_gate * gate_wide).astype(jnp.bfloat16)
    out_terms = jnp.einsum("sci,id->scd", hidden, full_out, preferred_element_type=single)
    mixed_part = lax.psum_scatter(
        out_terms.astype(jnp.bfloat16), "tp", scatter_dimension=2, tiled=True
    ).astype(jnp.float32)
    own_cols = lax.dynamic_slice_in_dim(x_float, tp_rank * slice_width, slice_width, 2)
    mixed = (own_cols + mixed_part).astype(jnp.bfloat16)
    grad_out_local = jnp.einsum("sci,scd->id", hidden, cotangent, preferred_element_type=single)
    d_hidden = jnp.einsum("scd,id->sci", cotangent, full_out, preferred_element_type=single)
    grad_gate_local = jnp.sum(d_hidden * gated_val * inv_gate, axis=(0, 1))
    d_scaled = d_hidden * gate_wide
    row_dot = lax.psum(jnp.sum(d_scaled * gated_val, axis=-1), "tp")
    d_gated = inv_gate * d_scaled - gated_val * inv_gate**3 * (row_dot / INNER)[..., None]
    d_yflat = d_gated * z_part * gate_sig
    d_zpart = d_gated * y_flat * gate_sig * (1.0 + z_part * (1.0 - gate_sig))
    d_yheads = d_yflat.reshape(seqs_here, block_len, heads_here, HEADDIM)
    d_into = jnp.sum(d_yheads * carried_read, axis=-1)
    weighted = d_yheads * into_scale[..., None]
    d_state_in = jnp.einsum("bthp,btn->bhpn", weighted, c_mat, precision=highest)
    d_c_extra = jnp.einsum("bthp,bhpn->btn", weighted, state_in, precision=highest)
    grad_skip_local = jnp.sum(d_yheads * x_heads, axis=(0, 1, 3))
    _, later_grad = entering((decay_total, d_state_in), "ctx", chain_pair, identity, True)
    d_decay = jnp.sum(later_grad * state_in, axis=(-2, -1))
    g_heads, g_bmat, g_cmat, g_raw, g_bias, g_alog = ssd_pull(
        (d_yheads, d_into, d_decay, later_grad)
    )
    g_heads = g_heads + d_yheads * skip_wide
    d_bc_total = lax.psum(jnp.concatenate([g_bmat, g_cmat + d_c_extra], axis=-1), "tp")
    d_activated = jnp.concatenate(
        [g_heads.reshape(seqs_here, block_len, inner_here), d_bc_total], axis=-1
    )
    g_uval, g_rims, g_conv_w, g_conv_b = pre_pull(d_activated)
    back_rims = shifted(as_sent(g_rims), "ctx", -1).astype(g_rims.dtype)
    g_uval = jnp.concatenate(
        [g_uval[:, : block_len - rim_len], g_uval[:, block_len - rim_len :] + back_rims], axis=1
    )
    d_zx = jnp.stack([d_zpart, g_uval[..., :inner_here]], axis=2).astype(jnp.bfloat16)
    d_bc = g_uval[..., inner_here:].astype(jnp.bfloat16)
    d_dtraw = g_raw.astype(jnp.bfloat16)
    grad_zx_local = jnp.einsum("scd,sckf->dkf", normed, d_zx, preferred_element_type=single)
    grad_bc_local = jnp.einsum("scd,scn->dn", normed, d_bc, preferred_element_type=single)
    grad_dt_local = jnp.einsum("scd,sch->dh", normed, d_dtraw, preferred_element_type=single)
    d_norm_part = jnp.einsum("sckf,dkf->scd", d_zx, full_zx, preferred_element_type=single)
    d_norm_part = d_norm_part + jnp.einsum(
        "sch,dh->scd", d_dtraw, full_dt, preferred_element_type=single
    )
    d_normed = lax.psum_scatter(
        d_norm_part.astype(jnp.bfloat16), "tp", scatter_dimension=2, tiled=True
    ).astype(jnp.float32)
    bc_rows = lax.dynamic_slice_in_dim(full_bc, tp_rank * slice_width, slice_width, 0)
    d_normed = d_normed + jnp.einsum("scn,dn->scd", d_bc, bc_rows, preferred_element_type=single)
    hat_slice = lax.dynamic_slice_in_dim(x_hat, tp_rank * slice_width, slice_width, 2)
    gain_slice = lax.dynamic_slice_in_dim(
        in_gain.astype(single), tp_rank * slice_width, slice_width, 0
    )
    grad_in_local = jnp.sum(d_normed * hat_slice, axis=(0, 1))
    d_hat = d_normed * gain_slice
    full_dot = lax.psum(jnp.sum(d_hat * hat_slice, axis=-1), "tp")
    cot_slice = lax.dynamic_slice_in_dim(cotangent, tp_rank * slice_width, slice_width, 2).astype(
        single
    )
    grad_tokens = cot_slice + inv_rms * (d_hat - hat_slice * (full_dot / D)[..., None])
    local_grads = (grad_zx_local, grad_bc_local, grad_dt_local, grad_out_local)
    grad_zx, grad_bc, grad_dt, grad_wout = (
        lax.psum_scatter(local_grads[0], ("fsdp", "ctx"), scatter_dimension=0, tiled=True),
        lax.psum_scatter(local_grads[1], ("fsdp", "ctx"), scatter_dimension=0, tiled=True),
        lax.psum_scatter(local_grads[2], ("fsdp", "ctx"), scatter_dimension=0, tiled=True),
        lax.psum_scatter(local_grads[3], ("fsdp", "ctx"), scatter_dimension=1, tiled=True),
    )
    small_grads = lax.psum(
        (grad_in_local, grad_gate_local, g_bias, g_alog, grad_skip_local, g_conv_w, g_conv_b),
        ("fsdp", "ctx"),
    )
    grad_in_gain, grad_gate, grad_bias, grad_alog, grad_skip, grad_convw, grad_convb = small_grads
    return (
        mixed,
        grad_tokens,
        grad_in_gain,
        grad_zx,
        grad_bc,
        grad_dt,
        grad_bias,
        grad_alog,
        grad_skip,
        grad_convw[:, :inner_here],
        grad_convb[:inner_here],
        grad_convw[:, inner_here:],
        grad_convb[inner_here:],
        grad_gate,
        grad_wout,
    )


def solution(mesh):
    return jax.shard_map(
        per_device,
        mesh=mesh,
        in_specs=(
            P("fsdp", "ctx", None),
            P("fsdp", "ctx"),
            P(),
            P(("fsdp", "ctx"), None, "tp"),
            P(("fsdp", "ctx"), None),
            P(("fsdp", "ctx"), "tp"),
            P("tp"),
            P("tp"),
            P("tp"),
            P(None, "tp"),
            P("tp"),
            P(),
            P(),
            P("tp"),
            P("tp", ("fsdp", "ctx")),
            P("fsdp", "ctx", None),
        ),
        out_specs=(
            P("fsdp", "ctx", "tp"),
            P("fsdp", "ctx", "tp"),
            P("tp"),
            P(("fsdp", "ctx"), None, "tp"),
            P(("fsdp", "ctx"), None),
            P(("fsdp", "ctx"), "tp"),
            P("tp"),
            P("tp"),
            P("tp"),
            P(None, "tp"),
            P("tp"),
            P(),
            P(),
            P("tp"),
            P("tp", ("fsdp", "ctx")),
        ),
        check_vma=False,
    )
```

profile of v0, /device:TPU:0, one launch (start us, length us, event | category | flops | bytes accessed | tf_op | source)
XLA Modules:
  0.0 1017.4 jit_solution(4566526465634261421)
XLA Ops:
  10.5 32.8 %all-gather.2 = bf16[8,192,12]{1,2,0:T(8,128)(2,1)S(1)} all-gather(bf16[1,192,12]{1,2,0:T(8,128)(2,1)} %bitcast.278), channel_id=1, replica_groups=mesh['fsdp'=2,'ctx'=4,'tp'=4] {'fsdp','ctx'}, dimensions={0}, use_global_device_ids=true | all-gather | bytes 41472 | tf_op jit(solution)/shard_map/all_gather | solution.py:116
  52.8 39.7 %all_gather.31 = bf16[1536,256]{1,0:T(8,128)(2,1)S(1)} all-gather(bf16[192,256]{1,0:T(8,128)(2,1)S(1)} %copy-done.27), channel_id=1, replica_groups=mesh['fsdp'=2,'ctx'=4,'tp'=4] {'fsdp','ctx'}, dimensions={0}, use_global_device_ids=true | all-gather | bytes 884736 | tf_op jit(solution)/shard_map/all_gather | solution.py:115
  96.4 9.0 all-gather.8.cloned.1.call-done
  105.3 8.0 fusion.27
  142.2 12.9 %all_gather.33 = f32[4,4,12]{2,1,0:T(4,128)S(1)} all-gather(f32[1,4,12]{2,1,0:T(4,128)S(1)} %bitcast_multiply_fusion.7), channel_id=1, replica_groups=mesh['fsdp'=2,'ctx'=4,'tp'=4] {'ctx'}, dimensions={0}, use_global_device_ids=true | all-gather | bytes 960 | tf_op jit(solution)/shard_map/all_gather | solution.py:26
  161.9 95.3 %all-gather.12.cloned.1.call-done = f32[16,12,64,128]{3,2,1,0:T(8,128)} async-done(((f32[4,12,64,128]{3,2,1,0:T(8,128)}), f32[16,12,64,128]{3,2,1,0:T(8,128)}) %all-gather.12.cloned.1.call-update) | async-done | bytes 6291472 | tf_op jit(solution)/shard_map/all_gather | solution.py:26
  261.5 17.9 %multiply_reduce_fusion.11 = (f32[4,256]{1,0:T(4,128)S(1)}, f32[4,256,12,64]{1,3,2,0:T(8,128)}) fusion(f32[4,256,12,64]{1,3,2,0:T(8,128)} %bitcast.254, f32[4,256,12,64]{1,3,2,0:T(8,128)S(1)} %bitcast.239, f32[12]{0:T(128)S(1)} %copy-done.67, f32[4,256,12,64]{1,3,2,0:T(8,128)S(1)} %fusion.73, f32[4,256,12]{1,2,0:T(8,128)S(1)} %get-tuple-element.272, ...), kind=kOutput, calls=%fused_computation.90 | convolution fusion | flops 2440297472 | bytes 15093808 | tf_op jit(solution)/shard_map/jvp(btsh,bshp->bthp)/dot_general | solution.py:65
  289.7 20.0 %all-gather.10.cloned.1.call-done = bf16[768,1536]{0,1:T(8,128)(2,1)} async-done(((bf16[768,192]{0,1:T(8,128)(2,1)}), bf16[768,1536]{0,1:T(8,128)(2,1)}) %all-gather.10.cloned.1.call-update) | async-done | bytes 2359312 | tf_op jit(solution)/shard_map/all_gather | solution.py:117
  309.7 10.8 %multiply_reduce_fusion.7 = (f32[768]{0:T(1024)}, f32[4,256]{1,0:T(4,128)S(1)}, f32[4,256,768]{2,1,0:T(8,128)}, f32[4,256,768]{2,1,0:T(8,128)}) fusion(f32[4,256]{1,0:T(4,128)S(1)} %get-tuple-element.278, f32[768]{0:T(1024)S(1)} %convert_element_type.95, f32[4,256,768]{2,1,0:T(8,128)} %copy.148, f32[4,256,2,768]{3,1,2,0:T(8,128)} %copy-done.11, ...), kind=kOutput, calls=%fused_computation.84 | convolution fusion | flops 2424568064 | bytes 18102272 | tf_op jit(solution)/shard_map/scd,id->sci/dot_general | solution.py:170
  320.5 16.7 %psum.78 = f32[4,256]{1,0:T(4,128)S(1)} all-reduce(f32[4,256]{1,0:T(4,128)S(1)} %get-tuple-element.215), channel_id=1, replica_groups=mesh['fsdp'=2,'ctx'=4,'tp'=4] {'tp'}, use_global_device_ids=true, to_apply=%region_9.10 | all-reduce | flops 1024 | bytes 8192 | tf_op jit(solution)/shard_map/psum | solution.py:173
  337.2 9.1 multiply_reduce_fusion.8
  363.2 23.2 %fusion.9 = (f32[4,256,12]{1,2,0:T(8,128)S(1)}, f32[4,256,12]{1,2,0:T(8,128)}, f32[4,256,12]{1,2,0:T(8,128)}, f32[4,256,256]{2,1,0:T(8,128)S(1)}) fusion(f32[4,256,12]{1,2,0:T(8,128)S(1)} %get-tuple-element.270, f32[4,256,256]{2,1,0:T(8,128)S(1)} %copy-done.21, f32[4,256,256]{2,1,0:T(8,128)S(1)} %get-tuple-element.269, f32[4,256,12]{1,2,0:T(8,128)S(1)} %bitcast.261, ...), kind=kOutput, calls=%fused_computation.16 | convolution fusion | flops 2462806016 | bytes 9945088 | tf_op jit(solution)/shard_map/transpose(jvp(btsh,bshp->bthp))/dot_general | solution.py:65
  390.4 79.9 %all-gather.14.cloned.1.call-done = f32[16,12,64,128]{3,2,1,0:T(8,128)} async-done(((f32[4,12,64,128]{3,2,1,0:T(8,128)}), f32[16,12,64,128]{3,2,1,0:T(8,128)}) %all-gather.14.cloned.1.call-update) | async-done | bytes 6291472 | tf_op jit(solution)/shard_map/all_gather | solution.py:26
  512.7 12.9 %fusion.33 = f32[4,256,12,64]{1,3,2,0:T(8,128)} fusion(f32[4,256,12,64]{1,3,2,0:T(8,128)S(1)} %bitcast.246, f32[4,256,12,64]{1,3,2,0:T(8,128)S(1)} %get-tuple-element.291, f32[4,12,64,256]{3,2,1,0:T(8,128)S(1)} %bitcast.247, f32[4,256,12]{1,2,0:T(8,128)S(1)} %copy-done.29, f32[4,256,256]{2,1,0:T(8,128)S(1)} %copy-done.22, ...), kind=kOutput, calls=%fused_computation.67 | convolution fusion | flops 2434793472 | bytes 15089712 | tf_op jit(solution)/shard_map/transpose(jvp(btsh,bshp->bthp))/dot_general | solution.py:65
  531.3 9.9 reduce-window.16
  542.7 10.7 %fusion.122 = (f32[1024]{0:T(1024)S(1)}, f32[1024]{0:T(1024)S(1)}, f32[1024]{0:T(1024)S(1)}, f32[1024]{0:T(1024)S(1)}, f32[1024]{0:T(1024)S(1)}, /*index=5*/f32[4,256,1024]{2,1,0:T(8,128)S(1)}) fusion(f32[4,256,256]{2,1,0:T(8,128)} %copy-done.10, f32[4,256,768]{2,1,0:T(8,128)} %copy-done.1, f32[4,256]{1,0:T(4,128)S(1)} %get-tuple-element.281, ...), kind=kLoop, calls=%fused_computation.221 | loop fusion | flops 25160704 | bytes 29396992 | tf_op jit(solution)/shard_map/transpose(jvp())/reduce_sum | solution.py:46
  558.8 9.5 pad_add_fusion
  598.3 10.0 convolution_bitcast_fusion
  609.0 7.9 convolution_bitcast_fusion.1
  640.3 35.0 %reduce-scatter.21.cloned.1.call-done = bf16[384,1024]{1,0:T(8,128)(2,1)} async-done(((bf16[1536,1024]{1,0:T(8,128)(2,1)}), bf16[384,1024]{1,0:T(8,128)(2,1)}) %reduce-scatter.21.cloned.1.call-update) | async-done | bytes 786448
  680.3 40.1 %all-reduce.10 = (f32[384]{0:T(512)}, f32[12]{0:T(128)}, f32[12]{0:T(128)}, f32[12]{0:T(128)}, f32[4,1024]{1,0:T(4,128)S(1)}, /*index=5*/f32[1024]{0:T(1024)S(1)}, f32[768]{0:T(1024)}) all-reduce(f32[384]{0:T(512)S(1)} %get-tuple-element.212, f32[12]{0:T(128)S(1)} %get-tuple-element.255, ...), channel_id=1, replica_groups=mesh['fsdp'=2,'ctx'=4,'tp'=4] {'fsdp','ctx'}, use_global_device_ids=true, to_apply=%region_26.27 | all-reduce | flops 6308 | bytes 50464 | tf_op jit(solution)/shard_map/psum | solution.py:231
  731.4 111.8 %reduce-scatter.13.cloned.1.call-done = f32[192,2,768]{2,0,1:T(8,128)} async-done(((f32[1536,2,768]{2,0,1:T(8,128)}), f32[192,2,768]{2,0,1:T(8,128)}) %reduce-scatter.13.cloned.1.call-update) | async-done | bytes 1179664 | tf_op jit(solution)/shard_map/reduce_scatter | solution.py:226
  846.4 95.4 %reduce-scatter.17.cloned.1.call-done = f32[768,192]{0,1:T(8,128)} async-done(((f32[768,1536]{0,1:T(8,128)}), f32[768,192]{0,1:T(8,128)}) %reduce-scatter.17.cloned.1.call-update) | async-done | bytes 589840 | tf_op jit(solution)/shard_map/reduce_scatter | solution.py:229
  941.8 68.6 %reduce-scatter.15.cloned.1.call-done = f32[192,256]{1,0:T(8,128)} async-done(((f32[1536,256]{1,0:T(8,128)}), f32[192,256]{1,0:T(8,128)}) %reduce-scatter.15.cloned.1.call-update) | async-done | bytes 196624 | tf_op jit(solution)/shard_map/reduce_scatter | solution.py:227
  (293 shorter events, 219.7 us)
Async XLA Ops:
  7.2 98.1 %all-gather.8.cloned.1.call-start = ((), (), s32[]{:S(2)}) async-start(), calls=%async_computation.6 | async-start | bytes 5308416 | tf_op jit(solution)/shard_map/all_gather | solution.py:114
  9.2 248.0 %all-gather.12.cloned.1.call-start = ((), (), s32[]{:S(2)}) async-start(), calls=%async_computation.12 | async-start | bytes 7864320 | tf_op jit(solution)/shard_map/all_gather | solution.py:26
  9.9 95.4 %copy-start.54 = (f32[1536]{0:T(1024)}, f32[1536]{0:T(1024)S(1)}, u32[]{:S(2)}) copy-start(f32[1536]{0:T(1024)S(1)} %convert_element_type.85) | copy-start | bytes 18436
  51.9 69.7 %copy-start.40 = (f32[1,1024]{1,0:T(1,128)}, f32[1,1024]{1,0:T(1,128)S(1)}, u32[]{:S(2)}) copy-start(f32[1,1024]{1,0:T(1,128)S(1)} %get-tuple-element.273) | copy-start | bytes 12292
  51.9 69.7 %copy-start.42 = (f32[1,1024]{1,0:T(1,128)}, f32[1,1024]{1,0:T(1,128)S(1)}, u32[]{:S(2)}) copy-start(f32[1,1024]{1,0:T(1,128)S(1)} %get-tuple-element.274) | copy-start | bytes 12292
  52.0 69.7 %copy-start.44 = (f32[1,1024]{1,0:T(1,128)}, f32[1,1024]{1,0:T(1,128)S(1)}, u32[]{:S(2)}) copy-start(f32[1,1024]{1,0:T(1,128)S(1)} %get-tuple-element.275) | copy-start | bytes 12292
  52.7 88.7 %copy-start.37 = (f32[4,256]{1,0:T(4,128)}, f32[4,256]{1,0:T(4,128)S(1)}, u32[]{:S(2)}) copy-start(f32[4,256]{1,0:T(4,128)S(1)} %get-tuple-element.280) | copy-start | bytes 12292
  52.8 310.4 %copy-start.28 = (f32[4,256,12]{1,2,0:T(8,128)}, f32[4,256,12]{1,2,0:T(8,128)S(1)}, u32[]{:S(2)}) copy-start(f32[4,256,12]{1,2,0:T(8,128)S(1)} %get-tuple-element.270) | copy-start | bytes 147460
  116.9 4.1 collective-permute-start
  140.4 169.3 %all-gather.10.cloned.1.call-start = ((), (), s32[]{:S(2)}) async-start(), calls=%async_computation.7 | async-start | bytes 2654208 | tf_op jit(solution)/shard_map/all_gather | solution.py:117
  141.1 329.2 %all-gather.14.cloned.1.call-start = ((), (), s32[]{:S(2)}) async-start(), calls=%async_computation.13 | async-start | bytes 7864320 | tf_op jit(solution)/shard_map/all_gather | solution.py:26
  142.0 221.2 %copy-start.18 = (f32[4,256,256]{2,1,0:T(8,128)}, f32[4,256,256]{2,1,0:T(8,128)S(1)}, u32[]{:S(2)}) copy-start(f32[4,256,256]{2,1,0:T(8,128)S(1)} %get-tuple-element.269) | copy-start | bytes 3145732
  142.0 221.2 %copy-start.23 = (pred[4,256,256]{2,1,0:T(8,128)(4,1)}, pred[4,256,256]{2,1,0:T(8,128)(4,1)S(1)}, u32[]{:S(2)}) copy-start(pred[4,256,256]{2,1,0:T(8,128)(4,1)S(1)} %get-tuple-element.268) | copy-start | bytes 786436
  142.0 345.4 %copy-start.51 = (f32[768]{0:T(1024)}, f32[768]{0:T(1024)S(1)}, u32[]{:S(2)}) copy-start(f32[768]{0:T(1024)S(1)} %convert_element_type.95) | copy-start | bytes 9220
  289.7 197.7 %copy-start.49 = (f32[4,256]{1,0:T(4,128)}, f32[4,256]{1,0:T(4,128)S(1)}, u32[]{:S(2)}) copy-start(f32[4,256]{1,0:T(4,128)S(1)} %get-tuple-element.278) | copy-start | bytes 12292
  356.0 186.7 %all-reduce.13.cloned.1.call-start = ((), (), s32[]{:S(2)}) async-start(), calls=%async_computation.8 | async-start | bytes 2097152 | tf_op jit(solution)/shard_map/psum | solution.py:189
  487.4 146.0 %reduce-scatter.19.cloned.1.call-start = ((), (), s32[]{:S(2)}) async-start(), calls=%async_computation.14 | async-start | bytes 3932160
  504.7 134.0 %reduce-scatter.23.cloned.1.call-start = ((), (), s32[]{:S(2)}) async-start(), calls=%async_computation.16 | async-start | bytes 884736
  569.3 6.6 collective-permute-start.1
  572.7 102.6 %reduce-scatter.21.cloned.1.call-start = ((), (), s32[]{:S(2)}) async-start(), calls=%async_computation.15 | async-start | bytes 3932160
  598.3 244.9 %reduce-scatter.13.cloned.1.call-start = ((), (), s32[]{:S(2)}) async-start(), calls=%async_computation.9 | async-start | bytes 10616832 | tf_op jit(solution)/shard_map/reduce_scatter | solution.py:226
  608.3 333.5 %reduce-scatter.17.cloned.1.call-start = ((), (), s32[]{:S(2)}) async-start(), calls=%async_computation.11 | async-start | bytes 5308416 | tf_op jit(solution)/shard_map/reduce_scatter | solution.py:229
  616.9 393.5 %reduce-scatter.15.cloned.1.call-start = ((), (), s32[]{:S(2)}) async-start(), calls=%async_computation.10 | async-start | bytes 1769472 | tf_op jit(solution)/shard_map/reduce_scatter | solution.py:227
  720.4 126.0 %copy-start.65 = (f32[1024]{0:T(1024)}, f32[1024]{0:T(1024)S(1)}, u32[]{:S(2)}) copy-start(f32[1024]{0:T(1024)S(1)} %get-tuple-element.250) | copy-start | bytes 12292
  (59 other events, 658.8 us)
Sparse Core Ops, SparseCore 0:
  10.7 94.5 all-gather.7
  140.5 116.6 all-gather.11
  259.3 50.3 all-gather.9
  356.1 114.1 all-gather.13
  487.5 34.2 all-reduce.12
  524.4 38.2 reduce-scatter.18
  572.9 62.7 reduce-scatter.22
  638.3 36.9 reduce-scatter.20
  678.9 164.2 reduce-scatter.12
  847.2 94.5 reduce-scatter.16
  945.8 64.5 reduce-scatter.14
where the time goes:
time: 1030 us; the launch traced here: 1020 us
  waiting for transfers between devices  517 us (50%)
  matrix products  163 us (16%)
  blocking collectives  155 us (15%)
  other arithmetic  89.5 us (9%)
  local copies, waits for them, and re-layouts  71 us (7%)
  between operations  15.6 us (2%)
    all_gather x2, waiting for transfers between devices, entering(): gathered = jax.tree.map(lambda a: lax.all_gather(a, axis), part)  175 us
    reduce_scatter x1, waiting for transfers between devices, per_device(): lax.psum_scatter(local_grads[0], ('fsdp', 'ctx'), scatter_dimension=0, ti...  112 us
    reduce_scatter x1, waiting for transfers between devices, per_device(): lax.psum_scatter(local_grads[3], ('fsdp', 'ctx'), scatter_dimension=1, ti...  95.4 us
    reduce_scatter x1, waiting for transfers between devices, per_device(): lax.psum_scatter(local_grads[1], ('fsdp', 'ctx'), scatter_dimension=0, ti...  68.6 us
    dot_general x3, matrix products, ssd_parts(): y_local = jnp.einsum('btsh,bshp->bthp', weights, x_heads, precision=highest)  54.1 us
    unnamed x152, local copies, waits for them, and re-layouts  40.2 us
    psum x1, blocking collectives, per_device(): lax.psum((grad_in_local, grad_gate_local, g_bias, g_alog, grad_skip_local...  40.1 us
    all_gather x1, blocking collectives, per_device(): lax.all_gather(w_bc, ('fsdp', 'ctx'), axis=0, tiled=True)  39.7 us
  transfers between devices with their start and end apart: 13, of which 9 were waited for; matrix products, arithmetic and copies ran while one was open for 24% of the time, Pallas kernels for 0%

commit v1 on v0

v1 whole, which is shorter than its diff:
```python
import functools

import jax
import jax.numpy as jnp
from jax import lax
from jax.experimental import pallas as pl
from jax.experimental.pallas import tpu as pltpu
from jax.sharding import PartitionSpec as P

D = 1536
HEADDIM = 64
STATE = 128
CONV = 4
INNER = 3072
NORM_EPS = 1e-05
LANES = 128
HALO = 16

bf16 = jnp.bfloat16
f32 = jnp.float32
NN = (((1,), (0,)), ((), ()))
NT = (((1,), (1,)), ((), ()))
TN = (((0,), (0,)), ((), ()))


def rotate(v, axis, steps):
    n = lax.axis_size(axis)
    return lax.ppermute(v, axis, [(i, (i + steps) % n) for i in range(n)])


def shift(v, axis, steps):
    n = lax.axis_size(axis)
    return lax.ppermute(v, axis, [(i, i + steps) for i in range(n) if 0 <= i + steps < n])


def flip(v, axis, mask):
    n = lax.axis_size(axis)
    return lax.ppermute(v, axis, [(i, i ^ mask) for i in range(n)])


def cube_sum(v, axis):
    mask = 1
    while mask < lax.axis_size(axis):
        v = v + flip(v, axis, mask)
        mask *= 2
    return v


def ring_gather(v):
    nc, nf = lax.axis_size("ctx"), lax.axis_size("fsdp")
    c, f = lax.axis_index("ctx"), lax.axis_index("fsdp")
    rows = v.shape[0]
    whole = jnp.zeros((rows * nc * nf, v.shape[1]), v.dtype)
    current = v
    for step in range(nc):
        if step:
            current = rotate(current, "ctx", 1)
        owner = lax.rem(c - step + nc, nc)
        piece = current
        for j in range(nf):
            if j:
                piece = rotate(piece, "fsdp", 1)
            place = lax.rem(f - j + nf, nf) * nc + owner
            whole = lax.dynamic_update_slice_in_dim(whole, piece, place * rows, 0)
    return whole


def ring_scatter(g):
    nc, nf = lax.axis_size("ctx"), lax.axis_size("fsdp")
    c, f = lax.axis_index("ctx"), lax.axis_index("fsdp")
    rows = g.shape[0] // (nc * nf)

    def piece(ff, cc):
        return lax.dynamic_slice_in_dim(g, (lax.rem(ff, nf) * nc + cc) * rows, rows, 0)

    total = None
    for step in range(1, nc + 1):
        cc = lax.rem(c - step + nc, nc)
        mine = piece(f, cc).astype(f32)
        for k in range(1, nf):
            mine = mine + rotate(piece(f + k, cc).astype(bf16), "fsdp", k).astype(f32)
        total = mine if total is None else total + mine
        if step < nc:
            total = rotate(total.astype(bf16), "ctx", 1).astype(f32)
    return total


def cube_scatter(v, axis):
    n, r = lax.axis_size(axis), lax.axis_index(axis)
    width = v.shape[1] // n
    held = [lax.dynamic_slice_in_dim(v, (r ^ k) * width, width, 1) for k in range(n)]
    mask = 1
    while mask < n:
        away = jnp.concatenate([held[i] for i in range(1, len(held), 2)], 1).astype(bf16)
        near = flip(away, axis, mask).astype(f32)
        kept = [held[i] for i in range(0, len(held), 2)]
        held = [k.astype(f32) + near[:, i * width : (i + 1) * width] for i, k in enumerate(kept)]
        mask *= 2
    return held[0]


def chain(parts, decay, reverse):
    n = lax.axis_size("ctx")
    entering, last = None, None
    for hop in range(1, n):
        out = parts
        if last is not None:
            out = (parts.astype(f32) + decay * last.astype(f32)).astype(bf16)
        pair = (n - hop, n - hop - 1) if reverse else (hop - 1, hop)
        last = lax.ppermute(out, "ctx", [pair])
        entering = last if entering is None else entering + last
    return entering


def dot(a, b, dims=NN):
    return lax.dot_general(a, b, dims, preferred_element_type=f32)


def split(v, terms):
    out = []
    for i in range(terms):
        t = v.astype(bf16)
        out.append(t)
        if i + 1 < terms:
            v = v - t.astype(f32)
    return out


def head_map(inner, transposed):
    shape = (inner, LANES) if transposed else (LANES, inner)
    ch = lax.broadcasted_iota(jnp.int32, shape, 0 if transposed else 1)
    hd = lax.broadcasted_iota(jnp.int32, shape, 1 if transposed else 0)
    return jnp.where(ch // HEADDIM == hd, 1.0, 0.0).astype(bf16)


def widen(v, inner):
    e = head_map(inner, False)
    return dot(jnp.concatenate(split(v, 2), 1), jnp.concatenate([e, e], 0))


def narrow(v, terms):
    e = head_map(v.shape[1], True)
    out = None
    for t in split(v, terms):
        s = dot(t, e)
        out = s if out is None else out + s
    return out


def tri_sum(tri, v, dims=NN):
    out = None
    for t in split(v, 3):
        s = dot(tri, t, dims)
        out = s if out is None else out + s
    return out


def triangle(q, strict=False):
    r = lax.broadcasted_iota(jnp.int32, (q, q), 0)
    c = lax.broadcasted_iota(jnp.int32, (q, q), 1)
    return jnp.where(c < r if strict else c <= r, 1.0, 0.0).astype(bf16)


def halves(v):
    lane = lax.broadcasted_iota(jnp.int32, v.shape, 1)
    zero = jnp.zeros_like(v)
    return jnp.where(lane < HEADDIM, v, zero), jnp.where(lane >= HEADDIM, v, zero)


def sigmoid(v):
    return 1.0 / (1.0 + jnp.exp(-v))


def project_kernel(nx, start, w, taps, bias, head_par, *refs, inner, conv):
    u_ref, pre_ref, act_ref, xdt_ref, dtl_ref, state_ref, dec_ref = refs[-7:]
    q = start.shape[0]
    u = dot(nx[...], w[...])
    u_ref[...] = u[:, :conv].astype(bf16)
    at = lax.broadcasted_iota(jnp.int32, (q, 1), 0)
    begin = start[...]
    since = at - begin
    for lo in range(0, conv, LANES):
        cols = slice(lo, lo + LANES)
        ut = u[:, cols]
        acc = bias[0:1, cols] + taps[CONV - 1 : CONV, cols] * ut[HALO:]
        for j in range(1, CONV):
            window = ut[HALO - j : HALO - j + q]
            acc = acc + taps[CONV - 1 - j : CONV - j, cols] * jnp.where(since >= j, window, 0.0)
        pre_ref[:, cols] = acc.astype(bf16)
        act_ref[:, cols] = (acc * sigmoid(acc)).astype(bf16)
    v = u[HALO:, conv:] + head_par[0:1, :]
    dt = jnp.maximum(v, 0.0) + jnp.log1p(jnp.exp(-jnp.abs(v)))
    cum = tri_sum(triangle(q), -dt * jnp.exp(head_par[1:2, :]))
    dtl_ref[:, :LANES] = dt
    dtl_ref[:, LANES:] = cum
    end = cum[q - 1 : q, :]
    begin_last = begin[q - 1 : q, :]
    tail = jnp.where(begin == begin_last, jnp.exp(end - cum), 0.0)
    xh = act_ref[:, :inner].astype(f32)
    xdt = (xh * widen(dt, inner)).astype(bf16)
    xdt_ref[...] = xdt
    weighted = (xdt.astype(f32) * widen(tail, inner)).astype(bf16)
    b = act_ref[:, inner : inner + STATE]
    state_ref[...] = dot(b, weighted, TN).astype(bf16)
    total = jnp.where(begin_last < 0, jnp.exp(end), 0.0)
    dec_ref[...] = widen(jnp.broadcast_to(total, (8, LANES)), inner)[0:1]


def score_mask(begin_col, q):
    r = lax.broadcasted_iota(jnp.int32, (q, q), 0)
    c = lax.broadcasted_iota(jnp.int32, (q, q), 1)
    return (c <= r) & (c >= begin_col)


def score_mask_t(begin_row, q):
    r = lax.broadcasted_iota(jnp.int32, (q, q), 0)
    c = lax.broadcasted_iota(jnp.int32, (q, q), 1)
    return (r <= c) & (r >= begin_row)


def local_kernel(act, xdt, dtl, start, y_ref, *, inner):
    q = start.shape[0]
    b = act[:, inner : inner + STATE]
    c = act[:, inner + STATE : inner + 2 * STATE]
    scores = jnp.where(score_mask(start[...], q), dot(c, b, NT), 0.0)
    cum = dtl[:, LANES:]
    cum_t = cum.T
    for pair in range(inner // LANES):
        cols = slice(pair * LANES, (pair + 1) * LANES)
        weights = []
        for h in (2 * pair, 2 * pair + 1):
            gap = jnp.minimum(cum[:, h : h + 1] - cum_t[h : h + 1, :], 0.0)
            weights.append((jnp.exp(gap) * scores).astype(bf16))
        even, odd = halves(xdt[:, cols])
        y_ref[:, cols] = dot(weights[0], even) + dot(weights[1], odd)


def gate_sums_kernel(y_in, act, dtl, start, state, z, dh, rows, y_ref, sums_ref, *, inner):
    q = start.shape[0]
    c = act[:, inner + STATE : inner + 2 * STATE]
    into = widen(jnp.where(start[...] < 0, jnp.exp(dtl[:, LANES:]), 0.0), inner)
    y = y_in[...] + into * dot(c, state[...])
    y_ref[...] = y
    zz = z[...]
    gated = (y + rows[0:1, :] * act[:, :inner].astype(f32)) * (zz * sigmoid(zz))
    e = dh[...] * rows[1:2, :]
    ones = jnp.ones((8, inner), bf16)
    sq = dot(ones, (gated * gated).astype(bf16), NT)
    eg = dot(ones, (e * gated).astype(bf16), NT)
    row = lax.broadcasted_iota(jnp.int32, (8, q), 0)
    sums_ref[...] = jnp.where(row == 0, sq, eg)


def gate_kernel(y_in, act, dtl, start, z, dh, sums, rows, *refs, inner):
    hidden_ref, dy_ref, dz_ref, dstate_ref, grads_ref = refs[-5:]
    xh = act[:, :inner].astype(f32)
    y = y_in[...] + rows[0:1, :] * xh
    zz = z[...]
    sig = sigmoid(zz)
    silu = zz * sig
    gated = y * silu
    gain = rows[1:2, :]
    d_hidden = dh[...]
    sums_t = sums[...].T
    inv = lax.rsqrt(sums_t[:, 0:1] / INNER + NORM_EPS)
    back = sums_t[:, 1:2] * (inv * inv * inv) / INNER
    scaled = gated * inv
    hidden_ref[...] = (scaled * gain).astype(bf16)
    dg = inv * (d_hidden * gain) - gated * back
    dy = (dg * silu).astype(bf16)
    dy_ref[...] = dy
    dz_ref[...] = (dg * y * sig * (1.0 + zz * (1.0 - sig))).astype(bf16)
    gate_row = jnp.sum(d_hidden * scaled, axis=0, keepdims=True)
    dy_wide = dy.astype(f32)
    skip_row = jnp.sum(dy_wide * xh, axis=0, keepdims=True)
    row = lax.broadcasted_iota(jnp.int32, (8, inner), 0)
    grads_ref[...] = jnp.where(row == 0, gate_row, jnp.where(row == 1, skip_row, 0.0))
    into = widen(jnp.where(start[...] < 0, jnp.exp(dtl[:, LANES:]), 0.0), inner)
    c = act[:, inner + STATE : inner + 2 * STATE]
    dstate_ref[...] = dot(c, (into * dy_wide).astype(bf16), TN).astype(bf16)


def local_back_kernel(act, xdt, dtl, start, start_row, dy, state, dx_ref, dbc_ref, *, inner):
    q = start.shape[0]
    b = act[:, inner : inner + STATE]
    c = act[:, inner + STATE : inner + 2 * STATE]
    mask = score_mask_t(start_row[...], q)
    scores = jnp.where(mask, dot(b, c, NT), 0.0)
    cum = dtl[:, LANES:]
    cum_t = cum.T
    total = jnp.zeros((q, q), f32)
    for pair in range(inner // LANES):
        cols = slice(pair * LANES, (pair + 1) * LANES)
        dy_pair = dy[:, cols]
        x_even, x_odd = halves(xdt[:, cols])
        dy_even, dy_odd = halves(dy_pair)
        out = None
        for h, x_one, dy_one in ((2 * pair, x_even, dy_even), (2 * pair + 1, x_odd, dy_odd)):
            decay = jnp.exp(jnp.minimum(cum_t[h : h + 1, :] - cum[:, h : h + 1], 0.0))
            total = total + dot(x_one, dy_pair, NT) * decay
            term = dot((decay * scores).astype(bf16), dy_one)
            out = term if out is None else out + term
        dx_ref[:, cols] = out
    d_scores = jnp.where(mask, total, 0.0).astype(bf16)
    into = widen(jnp.where(start[...] < 0, jnp.exp(cum), 0.0), inner)
    weighted = (into * dy[...].astype(f32)).astype(bf16)
    dbc_ref[:, :STATE] = dot(d_scores, c)
    dbc_ref[:, STATE:] = dot(d_scores, b, TN) + dot(weighted, state[...], NT)


def conv_back_kernel(
    act, xdt, dtl, start, dy, y_in, dx, dbc, state, later, pre, u, dec, taps, rows, head_par, *refs, inner, conv
):
    du_ref, rim_ref, tap_ref, head_ref, dact = refs[-5:]
    q = start.shape[0]
    begin = start[...]
    b = act[:, inner : inner + STATE]
    dt, cum = dtl[:, :LANES], dtl[:, LANES:]
    end = cum[q - 1 : q, :]
    begin_last = begin[q - 1 : q, :]
    tail = widen(jnp.where(begin == begin_last, jnp.exp(end - cum), 0.0), inner)
    x_dt = xdt[...].astype(f32)
    d_y = dy[...].astype(f32)
    g = later[...]
    dx_tail = tail * dot(b, g)
    dact[:, inner : inner + STATE] = dbc[:, :STATE] + dot((x_dt * tail).astype(bf16), g, NT)
    dact[:, inner + STATE :] = dbc[:, STATE:]
    dx_local = dx[...]
    dx_all = dx_local + dx_tail
    dact[:, :inner] = dx_all * widen(dt, inner) + rows[0:1, :] * d_y
    flux_near = narrow(d_y * y_in[...] - x_dt * dx_local, 3)
    flux_tail = narrow(x_dt * dx_tail, 2)
    d_dt = narrow(dx_all * act[:, :inner].astype(f32), 2)
    through = jnp.sum(dec[...] * (g.astype(f32) * state[...].astype(f32)), axis=0, keepdims=True)
    through = narrow(jnp.broadcast_to(through, (8, inner)), 2)[0:1]
    d_log = tri_sum(triangle(q), flux_near, TN) + tri_sum(triangle(q, True), flux_tail) + through
    rate = jnp.exp(head_par[1:2, :])
    d_raw = (d_dt - rate * d_log) * (1.0 - jnp.exp(-dt))
    du_ref[:, conv:] = d_raw.astype(bf16)
    bias_row = jnp.sum(d_raw, axis=0, keepdims=True)
    log_row = -jnp.sum(d_log * dt * rate, axis=0, keepdims=True)
    row = lax.broadcasted_iota(jnp.int32, (8, LANES), 0)
    head_ref[...] = jnp.where(row == 0, bias_row, jnp.where(row == 1, log_row, 0.0))
    since = lax.broadcasted_iota(jnp.int32, (q, 1), 0) - begin
    for lo in range(0, conv, LANES):
        cols = slice(lo, lo + LANES)
        p = pre[:, cols].astype(f32)
        sig = sigmoid(p)
        dp = dact[:, cols] * (sig * (1.0 + p * (1.0 - sig)))
        ut = u[:, cols].astype(f32)
        zeros = jnp.zeros((HALO, LANES), f32)
        total = jnp.concatenate([zeros, taps[CONV - 1 : CONV, cols] * dp], 0)
        tap_rows = [jnp.sum(dp * ut[HALO:], axis=0, keepdims=True)]
        for j in range(1, CONV):
            masked = jnp.where(since >= j, dp, 0.0)
            tap_rows.append(jnp.sum(masked * ut[HALO - j : HALO - j + q], axis=0, keepdims=True))
            moved = jnp.concatenate([zeros, taps[CONV - 1 - j : CONV - j, cols] * masked, zeros], 0)
            total = total + moved[j : j + q + HALO]
        du_ref[:, cols] = total[HALO:].astype(bf16)
        rim_ref[:, cols] = total[:HALO].astype(bf16)
        out = jnp.sum(dp, axis=0, keepdims=True)
        for j in range(CONV):
            out = jnp.where(row == CONV - 1 - j, tap_rows[j], jnp.where(row == CONV, out, 0.0) if j == 0 else out)
        tap_ref[:, cols] = out


def call(kernel, first, count, ins, outs, shared=(), scratch=(), flops=0, moved=0, into=None):
    def spec(shape, base):
        block = (None,) + tuple(shape[1:])
        rest = (0,) * (len(shape) - 1)
        return pl.BlockSpec(block, lambda s: (s + base,) + rest)

    in_specs = [spec(a.shape, o) for a, o in ins]
    in_specs += [pl.BlockSpec(a.shape, lambda s, n=a.ndim: (0,) * n) for a in shared]
    operands = [a for a, _ in ins] + list(shared)
    aliases = {}
    if into is not None:
        for i, buf in enumerate(into):
            if buf is not None:
                aliases[len(operands)] = i
                operands.append(buf)
                in_specs.append(pl.BlockSpec(memory_space=pl.ANY))
    return pl.pallas_call(
        kernel,
        grid=(count,),
        in_specs=in_specs,
        out_specs=[spec(s, first if whole else 0) for s, _, whole in outs],
        out_shape=[jax.ShapeDtypeStruct(s, d) for s, d, _ in outs],
        scratch_shapes=list(scratch),
        input_output_aliases=aliases,
        compiler_params=pltpu.CompilerParams(vmem_limit_bytes=48 * 2**20),
        cost_estimate=pl.CostEstimate(flops=flops, bytes_accessed=moved, transcendentals=0),
    )(*operands)


def drop(kernel, n_in, n_alias):
    def run(*refs):
        kernel(*refs[:n_in], *refs[n_in + n_alias :])

    return run


def per_device(
    tokens,
    segment_ids,
    in_gain,
    w_zx,
    w_bc,
    w_dt,
    dt_bias,
    a_log,
    skip_gain,
    conv_x,
    conv_x_bias,
    conv_bc,
    conv_bc_bias,
    gate_gain,
    w_out,
    cotangent,
):
    tp_count, tp_rank = lax.axis_size("tp"), lax.axis_index("tp")
    ctx_rank = lax.axis_index("ctx")
    seqs, q, width = tokens.shape
    inner = w_zx.shape[2]
    heads = w_dt.shape[1]
    conv = inner + 2 * STATE
    cols = width // tp_count
    n_tok = seqs * q
    chunks = 2 if seqs % 2 == 0 else 1
    per = seqs // chunks

    first_w = jnp.concatenate(
        [w_zx[:, 1, :], w_bc, jnp.pad(w_dt, ((0, 0), (0, LANES - heads)))], axis=1
    )
    halo = shift(tokens[:, q - 8 :, :], "ctx", 1)
    w_in = ring_gather(first_w)
    second_w = jnp.concatenate([w_zx[:, 0, :], w_out.T], axis=1)
    second_w, w_in = lax.optimization_barrier((second_w, w_in))
    w_rest = ring_gather(second_w)
    w_z, w_o = w_rest[:, :inner], w_rest[:, inner:]

    x_ext = jnp.concatenate([jnp.zeros_like(halo), halo, tokens], axis=1).astype(f32)
    inv_rms = lax.rsqrt(jnp.mean(x_ext * x_ext, axis=-1, keepdims=True) + NORM_EPS)
    nx = (x_ext * inv_rms * in_gain.astype(f32)).astype(bf16)
    inv_rms = inv_rms[:, HALO:]
    normed = nx[:, HALO:].reshape(n_tok, width)

    begin = segment_ids - ctx_rank * q
    start = begin[:, :, None]
    start_row = begin[:, None, :]
    taps = jnp.concatenate([conv_x, conv_bc], axis=1).astype(f32)
    bias = jnp.concatenate([conv_x_bias, conv_bc_bias]).astype(f32)[None]
    head_par = jnp.pad(jnp.stack([dt_bias, a_log]), ((0, 6), (0, LANES - heads)))
    rows = jnp.pad(jnp.stack([jnp.repeat(skip_gain, HEADDIM), gate_gain.astype(f32)]), ((0, 6), (0, 0)))

    shape = lambda *s: (seqs,) + s
    part = lambda *s: (per,) + s

    bulk = [None] * 5
    states, decs = [], []
    for g in range(chunks):
        have = 0 if g == 0 else 5
        o = g * per
        out = call(
            drop(functools.partial(project_kernel, inner=inner, conv=conv), 6, have),
            o,
            per,
            [(nx, o), (start, o)],
            [
                (shape(q + HALO, conv), bf16, True),
                (shape(q, conv), bf16, True),
                (shape(q, conv), bf16, True),
                (shape(q, inner), bf16, True),
                (shape(q, 2 * LANES), f32, True),
                (part(STATE, inner), bf16, False),
                (part(1, inner), f32, False),
            ],
            shared=(w_in, taps, bias, head_par),
            into=None if g == 0 else bulk,
            flops=2 * per * q * width * conv,
            moved=10 * per * q * conv,
        )
        bulk = list(out[:5])
        states.append(out[5])
        decs.append(out[6])
    u, pre, act, xdt, dtl = bulk
    entering = [chain(states[g], decs[g], False) for g in range(chunks)]

    y_local = call(
        functools.partial(local_kernel, inner=inner),
        0,
        seqs,
        [(act, 0), (xdt, 0), (dtl, 0), (start, 0)],
        [(shape(q, inner), f32, True)],
        flops=8 * seqs * q * q * inner,
        moved=8 * n_tok * inner,
    )[0]
    cot = cotangent.reshape(n_tok, width)
    z = dot(normed, w_z).reshape(seqs, q, inner)
    d_hidden = dot(cot, w_o).reshape(seqs, q, inner)

    state_in = jnp.concatenate(entering, axis=0)
    y_scan, sums = call(
        functools.partial(gate_sums_kernel, inner=inner),
        0,
        seqs,
        [(y_local, 0), (act, 0), (dtl, 0), (start, 0), (state_in, 0), (z, 0), (d_hidden, 0)],
        [(shape(q, inner), f32, True), (shape(8, q), f32, True)],
        shared=(rows,),
        flops=2 * n_tok * inner * 200,
        moved=16 * n_tok * inner,
    )
    sums = cube_sum(sums, "tp")

    bulk = [None] * 3
    d_states, gate_rows = [], []
    for g in range(chunks):
        have = 0 if g == 0 else 3
        out = call(
            drop(functools.partial(gate_kernel, inner=inner), 8, have),
            g * per,
            per,
            [(y_scan, g * per), (act, g * per), (dtl, g * per), (start, g * per), (z, g * per), (d_hidden, g * per), (sums, g * per)],
            [
                (shape(q, inner), bf16, True),
                (shape(q, inner), bf16, True),
                (shape(q, inner), bf16, True),
                (part(STATE, inner), bf16, False),
                (part(8, inner), f32, False),
            ],
            shared=(rows,),
            into=None if g == 0 else bulk,
            flops=2 * per * q * inner * 200,
            moved=20 * per * q * inner,
        )
        bulk = list(out[:3])
        d_states.append(out[3])
        gate_rows.append(jnp.sum(out[4], axis=0))
    hidden, d_y, d_z = bulk
    later = [chain(d_states[g], decs[g], True) for g in range(chunks)]

    hidden2 = hidden.reshape(n_tok, inner)
    dz2 = d_z.reshape(n_tok, inner)
    mixed_part = cube_scatter(dot(hidden2, w_o, NT), "tp")
    own = lax.dynamic_slice_in_dim(tokens.reshape(n_tok, width), tp_rank * cols, cols, 1).astype(f32)
    mixed = (own + mixed_part).astype(bf16).reshape(seqs, q, cols)
    grad_wo = ring_scatter(dot(cot, hidden2, TN))
    grad_wz = ring_scatter(dot(normed, dz2, TN))
    d_norm_z = dot(dz2, w_z, NT)

    dx_local, dbc_local = call(
        functools.partial(local_back_kernel, inner=inner),
        0,
        seqs,
        [(act, 0), (xdt, 0), (dtl, 0), (start, 0), (start_row, 0), (d_y, 0), (state_in, 0)],
        [(shape(q, inner), f32, True), (shape(q, 2 * STATE), f32, True)],
        flops=16 * seqs * q * q * inner,
        moved=12 * n_tok * inner,
    )

    bulk = [None] * 2
    tap_rows, head_rows = [], []
    for g in range(chunks):
        have = 0 if g == 0 else 2
        o = g * per
        out = call(
            drop(functools.partial(conv_back_kernel, inner=inner, conv=conv), 16, have),
            o,
            per,
            [(act, o), (xdt, o), (dtl, o), (start, o), (d_y, o), (y_scan, o), (dx_local, o), (dbc_local, o), (state_in, o), (later[g], 0), (pre, o), (u, o), (decs[g], 0)],
            [
                (shape(q, conv + LANES), bf16, True),
                (shape(HALO, conv), bf16, True),
                (part(8, conv), f32, False),
                (part(8, LANES), f32, False),
            ],
            shared=(taps, rows, head_par),
            scratch=[pltpu.VMEM((q, conv), f32)],
            into=None if g == 0 else bulk,
            flops=2 * per * q * inner * 800,
            moved=30 * per * q * inner,
        )
        bulk = list(out[:2])
        tap_rows.append(jnp.sum(out[2], axis=0))
        head_rows.append(jnp.sum(out[3], axis=0))
    du, rim = bulk
    rim = shift(rim[:, 8:, :], "ctx", -1)
    edge = du[:, q - 8 :, :conv].astype(f32) + rim.astype(f32)
    du = lax.dynamic_update_slice(du, edge.astype(bf16), (0, q - 8, 0))
    du2 = du.reshape(n_tok, conv + LANES)

    d_normed = cube_scatter(d_norm_z + dot(du2, w_in, NT), "tp")
    grad_in = ring_scatter(dot(normed, du2, TN))

    own_inv = inv_rms.reshape(n_tok, 1)
    hat = own * own_inv
    gain = lax.dynamic_slice_in_dim(in_gain, tp_rank * cols, cols, 0).astype(f32)
    gain_row = jnp.sum(d_normed * hat, axis=0)
    d_hat = d_normed * gain
    full_dot = cube_sum(jnp.sum(d_hat * hat, axis=-1).reshape(seqs, q), "tp").reshape(n_tok, 1)
    own_cot = lax.dynamic_slice_in_dim(cot, tp_rank * cols, cols, 1).astype(f32)
    grad_tokens = (own_cot + own_inv * (d_hat - hat * (full_dot / D))).reshape(seqs, q, cols)

    tap_sum, head_sum, gate_sum = sum(tap_rows), sum(head_rows), sum(gate_rows)
    shared_part = cube_sum(tap_sum[: CONV + 1, inner:], "tp").reshape(-1, LANES)
    pieces = [
        tap_sum[: CONV + 1, :inner].reshape(-1, LANES),
        shared_part,
        gate_sum[0].reshape(-1, LANES),
        jnp.pad(gate_sum[1].reshape(heads, HEADDIM).sum(1), (0, LANES - heads))[None],
        head_sum[:2],
        gain_row.reshape(-1, LANES),
    ]
    small = cube_sum(cube_sum(jnp.concatenate(pieces, 0), "fsdp"), "ctx")
    offsets = [0]
    for piece in pieces:
        offsets.append(offsets[-1] + piece.shape[0])
    got = [small[a:b] for a, b in zip(offsets[:-1], offsets[1:])]
    conv_own = got[0].reshape(CONV + 1, inner)
    conv_all = got[1].reshape(CONV + 1, 2 * STATE)

    grad_bc = cube_sum(grad_in[:, inner:conv], "tp")
    return (
        mixed,
        grad_tokens,
        got[5].reshape(cols),
        jnp.stack([grad_wz, grad_in[:, :inner]], axis=1),
        grad_bc,
        grad_in[:, conv : conv + heads],
        got[4][0, :heads],
        got[4][1, :heads],
        got[3][0, :heads],
        conv_own[:CONV],
        conv_own[CONV],
        conv_all[:CONV],
        conv_all[CONV],
        got[2].reshape(inner),
        grad_wo.T,
    )


def solution(mesh):
    return jax.shard_map(
        per_device,
        mesh=mesh,
        in_specs=(
            P("fsdp", "ctx", None),
            P("fsdp", "ctx"),
            P(),
            P(("fsdp", "ctx"), None, "tp"),
            P(("fsdp", "ctx"), None),
            P(("fsdp", "ctx"), "tp"),
            P("tp"),
            P("tp"),
            P("tp"),
            P(None, "tp"),
            P("tp"),
            P(),
            P(),
            P("tp"),
            P("tp", ("fsdp", "ctx")),
            P("fsdp", "ctx", None),
        ),
        out_specs=(
            P("fsdp", "ctx", "tp"),
            P("fsdp", "ctx", "tp"),
            P("tp"),
            P(("fsdp", "ctx"), None, "tp"),
            P(("fsdp", "ctx"), None),
            P(("fsdp", "ctx"), "tp"),
            P("tp"),
            P("tp"),
            P("tp"),
            P(None, "tp"),
            P("tp"),
            P(),
            P(),
            P("tp"),
            P("tp", ("fsdp", "ctx")),
        ),
        check_vma=False,
    )
```

time: 1030 us -> 454 us (0.44)
  waiting for transfers between devices: 517 us -> 137 us
  blocking collectives: 155 us -> 0 us
  matrix products: 163 us -> 35.9 us
  starting transfers between devices: 4.93 us -> 97.1 us
  Pallas kernels: 0 us -> 70.4 us
  other arithmetic: 89.5 us -> 56.3 us
  local copies, waits for them, and re-layouts: 71 us -> 45.4 us
  between operations: 15.6 us -> 2.58 us
    reduce_scatter x3 -> x0, waiting for transfers between devices: 276 us -> none  [the longest x1 112 us: per_device(): lax.psum_scatter(local_grads[0], ('fsdp', 'ctx'), scatter_dimension=0, ti...]
    all_gather x4 -> x0, waiting for transfers between devices: 204 us -> none  [the longest x2 175 us: entering(): gathered = jax.tree.map(lambda a: lax.all_gather(a, axis), part)]
    ppermute x2 -> x64, waiting for transfers between devices: 1.55 us -> 137 us  [the longest x35 95.5 us: rotate(): return lax.ppermute(v, axis, [(i, (i + steps) % n) for i in range(n)])]
    dot_general x24 -> x8, matrix products: 163 us -> 35.9 us  [dot(): return lax.dot_general(a, b, dims, preferred_element_type=f32)]
    ppermute x2 -> x64, starting transfers between devices: 3.76 us -> 97.1 us  [the longest x35 69.4 us: rotate(): return lax.ppermute(v, axis, [(i, (i + steps) % n) for i in range(n)])]
    all_gather x3 -> x0, blocking collectives: 85.4 us -> none  [the longest x1 39.7 us: per_device(): lax.all_gather(w_bc, ('fsdp', 'ctx'), axis=0, tiled=True)]
    pallas_call x0 -> x9, Pallas kernels: none -> 70.4 us  [call(): pl.pallas_call(kernel, grid=(count,), in_specs=in_specs, out_specs=[spec(...]
    psum x4 -> x0, blocking collectives: 69.6 us -> none  [the longest x1 40.1 us: per_device(): lax.psum((grad_in_local, grad_gate_local, g_bias, g_alog, grad_skip_local...]
  transfers between devices with their start and end apart: 13 -> 64, of which waited for: 9 -> 25; matrix products, arithmetic and copies ran while one was open for 24% -> 23% of each run, Pallas kernels for 0% -> 12%
where the time goes in v1:
time: 454 us; the launch traced here: 445 us
  waiting for transfers between devices  137 us (30%)
  starting transfers between devices  97.1 us (21%)
  Pallas kernels  70.4 us (16%)
  other arithmetic  56.3 us (12%)
  local copies, waits for them, and re-layouts  45.4 us (10%)
  matrix products  35.9 us (8%)
    ppermute x35, waiting for transfers between devices, rotate(): return lax.ppermute(v, axis, [(i, (i + steps) % n) for i in range(n)])  95.5 us
    pallas_call x9, Pallas kernels, call(): pl.pallas_call(kernel, grid=(count,), in_specs=in_specs, out_specs=[spec(...  70.4 us
    ppermute x35, starting transfers between devices, rotate(): return lax.ppermute(v, axis, [(i, (i + steps) % n) for i in range(n)])  69.4 us
    dot_general x8, matrix products, dot(): return lax.dot_general(a, b, dims, preferred_element_type=f32)  35.9 us
    ppermute x15, waiting for transfers between devices, flip(): return lax.ppermute(v, axis, [(i, i ^ mask) for i in range(n)])  23.8 us
    unnamed x157, local copies, waits for them, and re-layouts  13.3 us
    ppermute x12, starting transfers between devices, chain(): last = lax.ppermute(out, 'ctx', [pair])  12 us
    ppermute x15, starting transfers between devices, flip(): return lax.ppermute(v, axis, [(i, i ^ mask) for i in range(n)])  10.8 us
  transfers between devices with their start and end apart: 64, of which 25 were waited for; matrix products, arithmetic and copies ran while one was open for 23% of the time, Pallas kernels for 12%

profile of v1, /device:TPU:0, one launch (start us, length us, event | category | flops | bytes accessed | tf_op | source)
XLA Modules:
  0.0 444.8 jit_solution(6291667169654154960)
XLA Ops:
  32.5 9.1 %collective-permute-done.4 = bf16[192,1152]{1,0:T(8,128)(2,1)S(1)} collective-permute-done((bf16[192,1152]{1,0:T(8,128)(2,1)S(1)}, bf16[192,1152]{1,0:T(8,128)(2,1)S(1)}, u32[]{:S(2)}, u32[]{:S(2)}) %collective-permute-start.4) | collective-permute-done | bytes 442400 | tf_op jit(solution)/shard_map/ppermute | solution.py:28
  44.8 9.7 %collective-permute-done.6 = bf16[192,1152]{1,0:T(8,128)(2,1)S(1)} collective-permute-done((bf16[192,1152]{1,0:T(8,128)(2,1)S(1)}, bf16[192,1152]{1,0:T(8,128)(2,1)S(1)}, u32[]{:S(2)}, u32[]{:S(2)}) %collective-permute-start.6) | collective-permute-done | bytes 442400 | tf_op jit(solution)/shard_map/ppermute | solution.py:28
  56.6 7.2 %collective-permute-done.7 = bf16[192,1152]{1,0:T(8,128)(2,1)S(1)} collective-permute-done((bf16[192,1152]{1,0:T(8,128)(2,1)S(1)}, bf16[192,1152]{1,0:T(8,128)(2,1)S(1)}, u32[]{:S(2)}, u32[]{:S(2)}) %collective-permute-start.7) | collective-permute-done | bytes 442400 | tf_op jit(solution)/shard_map/ppermute | solution.py:28
  65.1 8.6 %shard_map.271 = (bf16[4,272,1024]{2,1,0:T(8,128)(2,1)}, bf16[4,256,1024]{2,1,0:T(8,128)(2,1)S(1)}, bf16[4,256,1024]{2,1,0:T(8,128)(2,1)}, bf16[4,256,768]{2,1,0...) custom-call(bf16[4,272,1536]{2,1,0:T(8,128)(2,1)} %fusion.2.refs_0_, ...), custom_call_target="tpu_custom_call" | custom-call | flops 1610612736 | bytes 5242880 | tf_op jit(solution)/shard_map/pallas_call | solution.py:383
  75.0 8.8 %shard_map.272 = (bf16[4,272,1024]{2,1,0:T(8,128)(2,1)}, bf16[4,256,1024]{2,1,0:T(8,128)(2,1)S(1)}, bf16[4,256,1024]{2,1,0:T(8,128)(2,1)}, bf16[4,256,768]{2,1,0...) custom-call(bf16[4,272,1536]{2,1,0:T(8,128)(2,1)} %fusion.2.refs_0_,, ...), custom_call_target="tpu_custom_call", output_to_operand_aliasing={{0}: (6, {}), {1}: (7, {}), {2}: (8, {}), {3}: (9, {}), {4}... | custom-call | flops 1610612736 | bytes 5242880 | tf_op jit(solution)/shard_map/pallas_call | solution.py:383
  87.1 5.3 %shard_map.273.y_in = f32[4,256,768]{2,1,0:T(8,128)} custom-call(bf16[4,256,1024]{2,1,0:T(8,128)(2,1)S(1)} %copy-done, bf16[4,256,768]{2,1,0:T(8,128)(2,1)S(1)} %get-tuple-element.60.xdt.refs_1_, f32[4,256,256]{2,1,0:T(8,128)S(1)} %get-tuple-element.61.dtl.refs_2_, s32[4,256,1]{2,1,0:T(8,128)S(1)} %copy-done.2), custom_call_target="tpu_custom_call" | custom-call | flops 1610612736 | bytes 6291456 | tf_op jit(solution)/shard_map/pallas_call | solution.py:383
  100.3 7.0 %collective-permute-done.17 = bf16[192,1536]{1,0:T(8,128)(2,1)S(1)} collective-permute-done((bf16[192,1536]{1,0:T(8,128)(2,1)S(1)}, bf16[192,1536]{1,0:T(8,128)(2,1)S(1)}, u32[]{:S(2)}, u32[]{:S(2)}) %collective-permute-start.17) | collective-permute-done | bytes 589856 | tf_op jit(solution)/shard_map/ppermute | solution.py:28
  107.3 15.1 %collective-permute-start.19 = (bf16[192,1536]{1,0:T(8,128)(2,1)S(1)}, bf16[192,1536]{1,0:T(8,128)(2,1)S(1)}, u32[]{:S(2)}, u32[]{:S(2)}) collective-permute-start(bf16[192,1536]{1,0:T(8,128)(2,1)S(1)} %collective-permute-done.17), channel_id=1, source_target_pairs={{0,4},{4,8},{8,12},{12,0},{1,5},{5,9},{9,13},{13,1},{2,6},{6,10},{... | collective-permute-start | bytes 1769480 | tf_op jit(solution)/shard_map/ppermute | solution.py:28
  124.8 5.9 %collective-permute-done.19 = bf16[192,1536]{1,0:T(8,128)(2,1)S(1)} collective-permute-done((bf16[192,1536]{1,0:T(8,128)(2,1)S(1)}, bf16[192,1536]{1,0:T(8,128)(2,1)S(1)}, u32[]{:S(2)}, u32[]{:S(2)}) %collective-permute-start.19) | collective-permute-done | bytes 589856 | tf_op jit(solution)/shard_map/ppermute | solution.py:28
  136.4 6.2 %collective-permute-done.20 = bf16[192,1536]{1,0:T(8,128)(2,1)S(1)} collective-permute-done((bf16[192,1536]{1,0:T(8,128)(2,1)S(1)}, bf16[192,1536]{1,0:T(8,128)(2,1)S(1)}, u32[]{:S(2)}, u32[]{:S(2)}) %collective-permute-start.20) | collective-permute-done | bytes 589856 | tf_op jit(solution)/shard_map/ppermute | solution.py:28
  157.0 6.8 %shard_map.274 = (f32[4,256,768]{2,1,0:T(8,128)}, f32[4,8,256]{2,1,0:T(8,128)S(1)}) custom-call(f32[4,256,768]{2,1,0:T(8,128)} %shard_map.273.y_in, bf16[4,256,1024]{2,1,0:T(8,128)(2,1)S(1)} %copy-done, f32[4,256,256]{2,1,0:T(8,128)S(1)} %get-tuple-element.61.dtl.refs_2_, s32[4,256,1]{2,1,0:T(8,128)S(1)} %copy-done.3, bf16[4,128,768]{2,1,0:T(8,128)(2,1)S(1)} %copy-done.10, ...), custom_call_target="tpu_custom_call" | custom-call | flops 314572800 | bytes 12582912 | tf_op jit(solution)/shard_map/pallas_call | solution.py:383
  202.7 9.3 %shard_map.277 = (f32[4,256,768]{2,1,0:T(8,128)}, f32[4,256,256]{2,1,0:T(8,128)S(1)}) custom-call(bf16[4,256,1024]{2,1,0:T(8,128)(2,1)} %get-tuple-element.59.act.refs_1_.refs_0_, bf16[4,256,768]{2,1,0:T(8,128)(2,1)S(1)} %copy-done.7, f32[4,256,256]{2,1,0:T(8,128)S(1)} %get-tuple-element.61.dtl.refs_2_, s32[4,256,1]{2,1,0:T(8,128)S(1)} %copy-done.5, ...), custom_call_target="tpu_custom_call" | custom-call | flops 3221225472 | bytes 9437184 | tf_op jit(solution)/shard_map/pallas_call | solution.py:383
  224.8 5.4 %collective-permute-start.58 = (bf16[192,768]{0,1:T(8,128)(2,1)S(1)}, bf16[192,768]{0,1:T(8,128)(2,1)S(1)}, u32[]{:S(2)}, u32[]{:S(2)}) collective-permute-start(bf16[192,768]{0,1:T(8,128)(2,1)S(1)} %fusion.45), channel_id=1, source_target_pairs={{0,4},{4,8},{8,12},{12,0},{1,5},{5,9},{9,13},{13,1},{2,6},{6,10},{... | collective-permute-start | bytes 884744 | tf_op jit(solution)/shard_map/ppermute | solution.py:28
  237.9 14.2 %collective-permute-done.58 = bf16[192,768]{0,1:T(8,128)(2,1)S(1)} collective-permute-done((bf16[192,768]{0,1:T(8,128)(2,1)S(1)}, bf16[192,768]{0,1:T(8,128)(2,1)S(1)}, u32[]{:S(2)}, u32[]{:S(2)}) %collective-permute-start.58) | collective-permute-done | bytes 294944 | tf_op jit(solution)/shard_map/ppermute | solution.py:28
  257.7 15.5 %collective-permute-start.60 = (bf16[192,768]{0,1:T(8,128)(2,1)S(1)}, bf16[192,768]{0,1:T(8,128)(2,1)S(1)}, u32[]{:S(2)}, u32[]{:S(2)}) collective-permute-start(bf16[192,768]{0,1:T(8,128)(2,1)S(1)} %fusion.44), channel_id=1, source_target_pairs={{0,4},{4,8},{8,12},{12,0},{1,5},{5,9},{9,13},{13,1},{2,6},{6,10},{... | collective-permute-start | bytes 884744 | tf_op jit(solution)/shard_map/ppermute | solution.py:28
  275.8 5.6 %collective-permute-done.60 = bf16[192,768]{0,1:T(8,128)(2,1)S(1)} collective-permute-done((bf16[192,768]{0,1:T(8,128)(2,1)S(1)}, bf16[192,768]{0,1:T(8,128)(2,1)S(1)}, u32[]{:S(2)}, u32[]{:S(2)}) %collective-permute-start.60) | collective-permute-done | bytes 294944 | tf_op jit(solution)/shard_map/ppermute | solution.py:28
  285.2 7.4 %collective-permute-done.30 = bf16[2,128,768]{2,1,0:T(8,128)(2,1)S(1)} collective-permute-done((bf16[2,128,768]{2,1,0:T(8,128)(2,1)S(1)}, bf16[2,128,768]{2,1,0:T(8,128)(2,1)S(1)}, u32[]{:S(2)}, u32[]{:S(2)}) %collective-permute-start.30) | collective-permute-done | bytes 393248 | tf_op jit(solution)/shard_map/ppermute | solution.py:110
  294.1 10.7 %shard_map.278 = (bf16[4,256,1152]{2,1,0:T(8,128)(2,1)}, bf16[4,16,1024]{2,1,0:T(8,128)(2,1)S(1)}, f32[2,8,1024]{2,1,0:T(8,128)S(1)}, f32[2,8,128]{2,1,0:T(8,128)S(1)}) custom-call(bf16[4,256,1024]{2,1,0:T(8,128)(2,1)} %get-tuple-element.59.act.refs_1_.refs_0_, bf16[4,256,768]{2,1,0:T(8,128)(2,1)S(1)} %copy-done.7, ...), custom_call_target="tpu_custom_call" | custom-call | flops 629145600 | bytes 11796480 | tf_op jit(solution)/shard_map/pallas_call | solution.py:383
  306.7 10.7 %shard_map.279 = (bf16[4,256,1152]{2,1,0:T(8,128)(2,1)}, bf16[4,16,1024]{2,1,0:T(8,128)(2,1)S(1)}, f32[2,8,1024]{2,1,0:T(8,128)S(1)}, f32[2,8,128]{2,1,0:T(8,128)S(1)}) custom-call(bf16[4,256,1024]{2,1,0:T(8,128)(2,1)} %get-tuple-element.59.act.refs_1_.refs_0_, bf16[4,256,768]{2,1,0:T(8,128)(2,1)S(1)} %copy-done.7, ...), custom_call_target="tpu_custom_call", output_to_operand_aliasing={{0}: (16, {}), {1}: (17, {})} | custom-call | flops 629145600 | bytes 11796480 | tf_op jit(solution)/shard_map/pallas_call | solution.py:383
  325.1 7.2 %convolution_bitcast_fusion = f32[1536,1152]{1,0:T(8,128)S(1)} fusion(bf16[4,256,1152]{2,1,0:T(8,128)(2,1)} %fusion.51, bf16[4,272,1536]{2,1,0:T(8,128)(2,1)} %fusion.2.refs_0_), kind=kOutput, calls=%fused_computation | convolution fusion | flops 3623878656 | bytes 12582912 | tf_op jit(solution)/shard_map/dot_general | solution.py:116
  335.3 7.2 %fusion.55 = f32[1024,1536]{1,0:T(8,128)S(1)} fusion(bf16[1024,1152]{1,0:T(8,128)(2,1)S(1)} %bitcast.118, bf16[1536,1152]{1,0:T(8,128)(2,1)} %constant_dynamic-update-slice_fusion.8.refs_2_), kind=kOutput, calls=%fused_computation.157 | convolution fusion | flops 3623878656 | bytes 12189696 | tf_op jit(solution)/shard_map/dot_general | solution.py:116
  360.7 9.1 %collective-permute-done.52 = bf16[192,1152]{1,0:T(8,128)(2,1)S(1)} collective-permute-done((bf16[192,1152]{1,0:T(8,128)(2,1)S(1)}, bf16[192,1152]{1,0:T(8,128)(2,1)S(1)}, u32[]{:S(2)}, u32[]{:S(2)}) %collective-permute-start.52) | collective-permute-done | bytes 442400 | tf_op jit(solution)/shard_map/ppermute | solution.py:28
  399.1 10.8 %collective-permute-done.33 = bf16[1024,384]{1,0:T(8,128)(2,1)S(1)} collective-permute-done((bf16[1024,384]{1,0:T(8,128)(2,1)S(1)}, bf16[1024,384]{1,0:T(8,128)(2,1)S(1)}, u32[]{:S(2)}, u32[]{:S(2)}) %collective-permute-start.33) | collective-permute-done | bytes 786464 | tf_op jit(solution)/shard_map/ppermute | solution.py:38
  421.3 7.2 %collective-permute-done.56 = f32[192,256]{1,0:T(8,128)} collective-permute-done((f32[192,256]{1,0:T(8,128)S(1)}, f32[192,256]{1,0:T(8,128)}, u32[]{:S(2)}, u32[]{:S(2)}) %collective-permute-start.56) | collective-permute-done | bytes 196640 | tf_op jit(solution)/shard_map/ppermute | solution.py:38
  (406 shorter events, 232.3 us)
Async XLA Ops:
  6.1 24.8 %collective-permute-start.1 = (bf16[192,1152]{1,0:T(8,128)(2,1)S(1)}, bf16[192,1152]{1,0:T(8,128)(2,1)S(1)}, u32[]{:S(2)}, u32[]{:S(2)}) collective-permute-start(bf16[192,1152]{1,0:T(8,128)(2,1)S(1)} %get-tuple-element.146), channel_id=1, source_target_pairs={{0,16},{16,0},{1,17},{17,1},{2,18},{18,2},{3,19},{19,3},{4,20},{20... | collective-permute-start | bytes 1327112 | tf_op jit(solution)/shard_map/ppermute | solution.py:28
  64.6 32.8 %collective-permute-start.14 = (bf16[192,1536]{1,0:T(8,128)(2,1)}, bf16[192,1536]{1,0:T(8,128)(2,1)}, u32[]{:S(2)}, u32[]{:S(2)}) collective-permute-start(bf16[192,1536]{1,0:T(8,128)(2,1)} %pad_maximum_fusion.5), channel_id=1, source_target_pairs={{0,16},{16,0},{1,17},{17,1},{2,18},{18,2},{3,19},{19,3},{4,20},{20... | collective-permute-start | bytes 1769480 | tf_op jit(solution)/shard_map/ppermute | solution.py:28
  65.1 29.0 %collective-permute-start.15 = (bf16[192,1536]{1,0:T(8,128)(2,1)}, bf16[192,1536]{1,0:T(8,128)(2,1)S(1)}, u32[]{:S(2)}, u32[]{:S(2)}) collective-permute-start(bf16[192,1536]{1,0:T(8,128)(2,1)} %pad_maximum_fusion.5), channel_id=1, source_target_pairs={{0,4},{4,8},{8,12},{12,0},{1,5},{5,9},{9,13},{13,1},{2,6},{6,10},{... | collective-permute-start | bytes 1769480 | tf_op jit(solution)/shard_map/ppermute | solution.py:28
  94.1 30.7 %collective-permute-start.16 = (bf16[192,1536]{1,0:T(8,128)(2,1)S(1)}, bf16[192,1536]{1,0:T(8,128)(2,1)S(1)}, u32[]{:S(2)}, u32[]{:S(2)}) collective-permute-start(bf16[192,1536]{1,0:T(8,128)(2,1)S(1)} %collective-permute-done.15), channel_id=1, source_target_pairs={{0,16},{16,0},{1,17},{17,1},{2,18},{18,2},{3,19},{19,3},{4,20},{20... | collective-permute-start | bytes 1769480 | tf_op jit(solution)/shard_map/ppermute | solution.py:28
  99.5 23.0 %collective-permute-start.13 = (bf16[2,128,768]{2,1,0:T(8,128)(2,1)S(1)}, bf16[2,128,768]{2,1,0:T(8,128)(2,1)S(1)}, u32[]{:S(2)}, u32[]{:S(2)}) collective-permute-start(bf16[2,128,768]{2,1,0:T(8,128)(2,1)S(1)} %fusion.34), channel_id=1, source_target_pairs={{8,12},{9,13},{10,14},{11,15},{24,28},{25,29},{26,30},{27,31}} | collective-permute-start | bytes 1179656 | tf_op jit(solution)/shard_map/ppermute | solution.py:110
  107.3 23.4 %collective-permute-start.19 = (bf16[192,1536]{1,0:T(8,128)(2,1)S(1)}, bf16[192,1536]{1,0:T(8,128)(2,1)S(1)}, u32[]{:S(2)}, u32[]{:S(2)}) collective-permute-start(bf16[192,1536]{1,0:T(8,128)(2,1)S(1)} %collective-permute-done.17), channel_id=1, source_target_pairs={{0,4},{4,8},{8,12},{12,0},{1,5},{5,9},{9,13},{13,1},{2,6},{6,10},{... | collective-permute-start | bytes 1769480 | tf_op jit(solution)/shard_map/ppermute | solution.py:28
  185.4 35.5 %collective-permute-start.57 = (bf16[192,768]{0,1:T(8,128)(2,1)}, bf16[192,768]{0,1:T(8,128)(2,1)}, u32[]{:S(2)}, u32[]{:S(2)}) collective-permute-start(bf16[192,768]{0,1:T(8,128)(2,1)} %get-tuple-element.134), channel_id=1, source_target_pairs={{0,16},{16,0},{1,17},{17,1},{2,18},{18,2},{3,19},{19,3},{4,20},{20... | collective-permute-start | bytes 884744 | tf_op jit(solution)/shard_map/ppermute | solution.py:28
  185.7 50.3 %collective-permute-start.59 = (bf16[192,768]{0,1:T(8,128)(2,1)}, bf16[192,768]{0,1:T(8,128)(2,1)}, u32[]{:S(2)}, u32[]{:S(2)}) collective-permute-start(bf16[192,768]{0,1:T(8,128)(2,1)} %get-tuple-element.137), channel_id=1, source_target_pairs={{0,16},{16,0},{1,17},{17,1},{2,18},{18,2},{3,19},{19,3},{4,20},{20... | collective-permute-start | bytes 884744 | tf_op jit(solution)/shard_map/ppermute | solution.py:28
  187.5 88.3 %collective-permute-start.61 = (bf16[192,768]{0,1:T(8,128)(2,1)}, bf16[192,768]{0,1:T(8,128)(2,1)}, u32[]{:S(2)}, u32[]{:S(2)}) collective-permute-start(bf16[192,768]{0,1:T(8,128)(2,1)} %get-tuple-element.136), channel_id=1, source_target_pairs={{0,16},{16,0},{1,17},{17,1},{2,18},{18,2},{3,19},{19,3},{4,20},{20... | collective-permute-start | bytes 884744 | tf_op jit(solution)/shard_map/ppermute | solution.py:28
  187.8 37.0 %collective-permute-start.28 = (bf16[2,128,768]{2,1,0:T(8,128)(2,1)}, bf16[2,128,768]{2,1,0:T(8,128)(2,1)}, u32[]{:S(2)}, u32[]{:S(2)}) collective-permute-start(bf16[2,128,768]{2,1,0:T(8,128)(2,1)} %get-tuple-element.80), channel_id=1, source_target_pairs={{12,8},{13,9},{14,10},{15,11},{28,24},{29,25},{30,26},{31,27}} | collective-permute-start | bytes 1179656 | tf_op jit(solution)/shard_map/ppermute | solution.py:110
  194.8 28.6 %collective-permute-start.41 = (bf16[192,768]{1,0:T(8,128)(2,1)}, bf16[192,768]{1,0:T(8,128)(2,1)}, u32[]{:S(2)}, u32[]{:S(2)}) collective-permute-start(bf16[192,768]{1,0:T(8,128)(2,1)} %get-tuple-element.138), channel_id=1, source_target_pairs={{0,16},{16,0},{1,17},{17,1},{2,18},{18,2},{3,19},{19,3},{4,20},{20... | collective-permute-start | bytes 884744 | tf_op jit(solution)/shard_map/ppermute | solution.py:28
  223.4 31.1 %collective-permute-start.43 = (bf16[192,768]{1,0:T(8,128)(2,1)S(1)}, bf16[192,768]{1,0:T(8,128)(2,1)S(1)}, u32[]{:S(2)}, u32[]{:S(2)}) collective-permute-start(bf16[192,768]{1,0:T(8,128)(2,1)S(1)} %copy-done.46), channel_id=1, source_target_pairs={{0,16},{16,0},{1,17},{17,1},{2,18},{18,2},{3,19},{19,3},{4,20},{20... | collective-permute-start | bytes 884744 | tf_op jit(solution)/shard_map/ppermute | solution.py:28
  224.8 27.3 %collective-permute-start.58 = (bf16[192,768]{0,1:T(8,128)(2,1)S(1)}, bf16[192,768]{0,1:T(8,128)(2,1)S(1)}, u32[]{:S(2)}, u32[]{:S(2)}) collective-permute-start(bf16[192,768]{0,1:T(8,128)(2,1)S(1)} %fusion.45), channel_id=1, source_target_pairs={{0,4},{4,8},{8,12},{12,0},{1,5},{5,9},{9,13},{13,1},{2,6},{6,10},{... | collective-permute-start | bytes 884744 | tf_op jit(solution)/shard_map/ppermute | solution.py:28
  231.5 24.3 %collective-permute-start.42 = (bf16[192,768]{1,0:T(8,128)(2,1)S(1)}, bf16[192,768]{1,0:T(8,128)(2,1)S(1)}, u32[]{:S(2)}, u32[]{:S(2)}) collective-permute-start(bf16[192,768]{1,0:T(8,128)(2,1)S(1)} %add_convert_fusion.5), channel_id=1, source_target_pairs={{0,4},{4,8},{8,12},{12,0},{1,5},{5,9},{9,13},{13,1},{2,6},{6,10},{... | collective-permute-start | bytes 884744 | tf_op jit(solution)/shard_map/ppermute | solution.py:28
  236.1 120.7 %collective-permute-start.63 = (bf16[192,768]{0,1:T(8,128)(2,1)}, bf16[192,768]{0,1:T(8,128)(2,1)}, u32[]{:S(2)}, u32[]{:S(2)}) collective-permute-start(bf16[192,768]{0,1:T(8,128)(2,1)} %get-tuple-element.135), channel_id=1, source_target_pairs={{0,16},{16,0},{1,17},{17,1},{2,18},{18,2},{3,19},{19,3},{4,20},{20... | collective-permute-start | bytes 884744 | tf_op jit(solution)/shard_map/ppermute | solution.py:28
  254.5 62.9 %collective-permute-start.45 = (bf16[192,768]{1,0:T(8,128)(2,1)S(1)}, bf16[192,768]{1,0:T(8,128)(2,1)S(1)}, u32[]{:S(2)}, u32[]{:S(2)}) collective-permute-start(bf16[192,768]{1,0:T(8,128)(2,1)S(1)} %copy-done.45), channel_id=1, source_target_pairs={{0,16},{16,0},{1,17},{17,1},{2,18},{18,2},{3,19},{19,3},{4,20},{20... | collective-permute-start | bytes 884744 | tf_op jit(solution)/shard_map/ppermute | solution.py:28
  257.7 23.8 %collective-permute-start.60 = (bf16[192,768]{0,1:T(8,128)(2,1)S(1)}, bf16[192,768]{0,1:T(8,128)(2,1)S(1)}, u32[]{:S(2)}, u32[]{:S(2)}) collective-permute-start(bf16[192,768]{0,1:T(8,128)(2,1)S(1)} %fusion.44), channel_id=1, source_target_pairs={{0,4},{4,8},{8,12},{12,0},{1,5},{5,9},{9,13},{13,1},{2,6},{6,10},{... | collective-permute-start | bytes 884744 | tf_op jit(solution)/shard_map/ppermute | solution.py:28
  275.8 107.5 %collective-permute-start.23 = (bf16[1024,768]{1,0:T(8,128)(2,1)}, bf16[1024,768]{1,0:T(8,128)(2,1)}, u32[]{:S(2)}, u32[]{:S(2)}) collective-permute-start(bf16[1024,768]{1,0:T(8,128)(2,1)} %pad_maximum_fusion.1), channel_id=1, source_target_pairs={{0,1},{1,0},{2,3},{3,2},{4,5},{5,4},{6,7},{7,6},{8,9},{9,8},{10,11... | collective-permute-start | bytes 4718600 | tf_op jit(solution)/shard_map/ppermute | solution.py:38
  281.5 25.2 %collective-permute-start.27 = (bf16[2,128,768]{2,1,0:T(8,128)(2,1)S(1)}, bf16[2,128,768]{2,1,0:T(8,128)(2,1)S(1)}, u32[]{:S(2)}, u32[]{:S(2)}) collective-permute-start(bf16[2,128,768]{2,1,0:T(8,128)(2,1)S(1)} %fusion.36), channel_id=1, source_target_pairs={{4,0},{5,1},{6,2},{7,3},{20,16},{21,17},{22,18},{23,19}} | collective-permute-start | bytes 1179656 | tf_op jit(solution)/shard_map/ppermute | solution.py:110
  292.6 26.3 %collective-permute-start.44 = (bf16[192,768]{1,0:T(8,128)(2,1)S(1)}, bf16[192,768]{1,0:T(8,128)(2,1)S(1)}, u32[]{:S(2)}, u32[]{:S(2)}) collective-permute-start(bf16[192,768]{1,0:T(8,128)(2,1)S(1)} %add_convert_fusion.4), channel_id=1, source_target_pairs={{0,4},{4,8},{8,12},{12,0},{1,5},{5,9},{9,13},{13,1},{2,6},{6,10},{... | collective-permute-start | bytes 884744 | tf_op jit(solution)/shard_map/ppermute | solution.py:28
  306.6 50.7 %collective-permute-start.62 = (bf16[192,768]{0,1:T(8,128)(2,1)}, bf16[192,768]{0,1:T(8,128)(2,1)}, u32[]{:S(2)}, u32[]{:S(2)}) collective-permute-start(bf16[192,768]{0,1:T(8,128)(2,1)} %fusion.42), channel_id=1, source_target_pairs={{0,4},{4,8},{8,12},{12,0},{1,5},{5,9},{9,13},{13,1},{2,6},{6,10},{... | collective-permute-start | bytes 884744 | tf_op jit(solution)/shard_map/ppermute | solution.py:28
  356.6 28.3 %collective-permute-start.32 = (bf16[1024,768]{1,0:T(8,128)(2,1)S(1)}, bf16[1024,768]{1,0:T(8,128)(2,1)}, u32[]{:S(2)}, u32[]{:S(2)}) collective-permute-start(bf16[1024,768]{1,0:T(8,128)(2,1)S(1)} %pad_maximum_fusion.2), channel_id=1, source_target_pairs={{0,1},{1,0},{2,3},{3,2},{4,5},{5,4},{6,7},{7,6},{8,9},{9,8},{10,11... | collective-permute-start | bytes 4718600 | tf_op jit(solution)/shard_map/ppermute | solution.py:38
  397.0 39.1 %collective-permute-start.24 = (bf16[1024,384]{1,0:T(8,128)(2,1)}, bf16[1024,384]{1,0:T(8,128)(2,1)}, u32[]{:S(2)}, u32[]{:S(2)}) collective-permute-start(bf16[1024,384]{1,0:T(8,128)(2,1)} %fusion.28), channel_id=1, source_target_pairs={{0,2},{1,3},{2,0},{3,1},{4,6},{5,7},{6,4},{7,5},{8,10},{9,11},{10,... | collective-permute-start | bytes 2359304 | tf_op jit(solution)/shard_map/ppermute | solution.py:38
  398.5 30.0 %collective-permute-start.56 = (f32[192,256]{1,0:T(8,128)S(1)}, f32[192,256]{1,0:T(8,128)}, u32[]{:S(2)}, u32[]{:S(2)}) collective-permute-start(f32[192,256]{1,0:T(8,128)S(1)} %slice_add_fusion.5), channel_id=1, source_target_pairs={{0,2},{1,3},{2,0},{3,1},{4,6},{5,7},{6,4},{7,5},{8,10},{9,11},{10,... | collective-permute-start | bytes 589832 | tf_op jit(solution)/shard_map/ppermute | solution.py:38
  (115 other events, 1527.7 us)
